TPU v7x, 256 devices: a whole 4x4x8 slice. The times are simulated.
256 devices in a mesh: sub: 2 (over core), row: 8 (over y_lo, x), col: 16 (over z, y_hi).
Axes of the slice: x: 4, y: 4 (y_hi: 2, y_lo: 2; y = y_hi * 2 + y_lo), z: 8, core: 2. Of those that a mesh axis runs over, the one named last changes fastest.
Arguments:
- initial: float32 [12, 16, 256, 4096], P(None, ('sub', 'row'), None, 'col'), may hold values from -1 to 6
- pattern: int32 [12, 16, 16], P(None, ('sub', 'row'), 'col'), may hold values from 0 to 1, as said below
- rmap: int32 [2, 8, 16], replicated, may hold values from 0 to 191, as said below
- child_update: float32 [2, 8, 16, 256, 4096], P('sub', 'row', None, None, 'col'), may hold values from -0.5 to 0.5
Outputs:
- factored: float32 [12, 16, 256, 4096], P(None, ('sub', 'row'), None, 'col')
Inputs may be any that keep to these rules, and one draw needn't show every extreme that they name: Within one child the 128 entries are distinct tile rows; in each block rmap[c, r, :] exactly two remainders modulo 16 appear 2 times, two never, the others once. pattern[p, p] = 1 for p < 16.
All inputs are finite; a program needn't handle non-finite values.
Results may differ from a plain program's by a relative error of at most 0.0001.
Values sent between devices are 32-bit elements; how exact they have to be, the bound alone decides.
A program may use at most 128 MiB of HBM per device.

v0:
```python
import jax
import jax.numpy as jnp
from jax import lax
from jax.sharding import PartitionSpec as P

CAP = 2


def spread(block, axis, holder):
    block = jnp.where(lax.axis_index(axis) == holder, block, jnp.zeros_like(block))
    return lax.psum(block, axis)


def slot_ranks(tile_map, owners):
    target = tile_map % owners
    index = jnp.arange(target.shape[0])
    earlier = (target[None, :] == target[:, None]) & (index[None, :] < index[:, None])
    return (target, jnp.sum(earlier.astype(jnp.int32), axis=1))


def right_solve(factor, stacked):
    tile = factor.shape[0]
    flat = lax.linalg.triangular_solve(
        factor, stacked.reshape(-1, tile), left_side=False, lower=True, transpose_a=True
    )
    return flat.reshape(stacked.shape)


def per_device(initial, pattern, rmap, child_update):
    owners = lax.axis_size("sub") * lax.axis_size("row")
    frows = initial.shape[0]
    owner_me = lax.axis_index(("sub", "row"))
    child = lax.axis_index("sub")
    proc_row = lax.axis_index("row")
    column_me = lax.axis_index("col")
    slot_ids = jnp.arange(CAP)
    owner_ids = jnp.arange(owners)
    own_map = rmap[child, proc_row]
    target, ranks = slot_ranks(own_map, owners)
    select = (
        (target[None, None, :] == owner_ids[:, None, None])
        & (ranks[None, None, :] == slot_ids[None, :, None])
    ).astype(jnp.float32)
    outgoing = jnp.einsum(
        "dsk,kab->dsab", select, child_update[0, 0], precision=lax.Precision.HIGHEST
    )
    incoming = lax.all_to_all(outgoing, ("sub", "row"), split_axis=0, concat_axis=0, tiled=True)
    all_maps = rmap.reshape(owners, owners)
    all_target, all_ranks = jax.vmap(lambda one: slot_ranks(one, owners))(all_maps)
    local_row = all_maps // owners
    placing = (
        (all_target == owner_me)[None, :, None, :]
        & (all_ranks[None, :, None, :] == slot_ids[None, None, :, None])
        & (local_row[None, :, None, :] == jnp.arange(frows)[:, None, None, None])
    )
    placing = jnp.sum(placing.astype(jnp.float32), axis=3)
    front = initial[:, 0] * pattern[:, 0, :, None].astype(jnp.float32)
    front = front + jnp.einsum("msj,sjab->mab", placing, incoming, precision=lax.Precision.HIGHEST)
    tile_row = jnp.arange(frows) * owners + owner_me
    for step in range(2):
        column = spread(front, "col", step)
        diag = spread(column[step // owners], ("sub", "row"), step % owners)
        factor = jnp.linalg.cholesky(diag)
        solved = right_solve(factor, column)
        panel = jnp.where(
            (tile_row == step)[:, None, None],
            factor[None],
            jnp.where((tile_row > step)[:, None, None], solved, jnp.zeros_like(solved)),
        )
        own_tile = lax.dynamic_index_in_dim(panel, column_me // owners, 0, keepdims=False)
        row_tile = spread(own_tile, ("sub", "row"), column_me % owners)
        update = jnp.einsum("mab,cb->mac", panel, row_tile, precision=lax.Precision.HIGHEST)
        lower = (column_me > step) & (tile_row > step)[:, None, None]
        front = jnp.where(column_me == step, panel, jnp.where(lower, front - update, front))
    return front[:, None]


def solution(mesh):
    return jax.shard_map(
        per_device,
        mesh=mesh,
        in_specs=(
            P(None, ("sub", "row"), None, "col"),
            P(None, ("sub", "row"), "col"),
            P(),
            P("sub", "row", None, None, "col"),
        ),
        out_specs=P(None, ("sub", "row"), None, "col"),
        check_vma=False,
    )
```

profile of v0, /device:TPU:130, one launch (start us, length us, event | category | flops | bytes accessed | tf_op | source)
XLA Modules:
  0.0 1267.2 jit_solution(1868014286174128155)
XLA Ops:
  8.1 7.7 fusion.2
  15.9 9.7 copy.61
  25.6 5.9 all-to-all-start
  34.6 105.7 %all-to-all-done = f32[16,2,256,256]{3,1,2,0:T(2,128)} async-done(((f32[16,2,256,256]{3,1,2,0:T(2,128)}), f32[16,2,256,256]{3,1,2,0:T(2,128)}, u32[]{:S(2)}, u32[]{:S(2)}) %all-to-all-start) | async-done | bytes 8388640 | tf_op jit(solution)/shard_map/all_to_all | solution.py:47
  140.3 13.4 %fusion.9 = f32[12,256,256]{2,0,1:T(8,128)} fusion(f32[16,2,256,256]{3,1,2,0:T(2,128)} %all-to-all-done, f32[12,16,2]{1,2,0:T(2,128)S(1)} %convert_reduce_fusion), kind=kOutput, calls=%fused_computation.22 | convolution fusion | flops 301989888 | bytes 11535872 | tf_op jit(solution)/shard_map/msj,sjab->mab/dot_general | solution.py:58
  153.7 4.9 copy.64
  158.6 4.1 broadcast_select_fusion.1
  162.7 179.0 %all-reduce.8.cloned.1.call-done = f32[12,256,256]{1,2,0:T(8,128)} async-done(((f32[12,256,256]{1,2,0:T(8,128)}), f32[12,256,256]{1,2,0:T(8,128)}) %all-reduce.8.cloned.1.call-update) | async-done | bytes 3145744 | tf_op jit(solution)/shard_map/psum | solution.py:11
  347.8 131.2 %all-reduce.10.cloned.1.call-done = f32[256,256]{0,1:T(8,128)} async-done(((f32[256,256]{0,1:T(8,128)}), f32[256,256]{0,1:T(8,128)}) %all-reduce.10.cloned.1.call-update) | async-done | bytes 262160 | tf_op jit(solution)/shard_map/psum | solution.py:11
  481.8 11.7 cholesky.130
  493.6 9.8 custom-call.13
  505.5 11.7 cholesky.147
  522.3 4.0 while.4
  526.9 20.7 %custom-call.14 = f32[2,128,128]{1,2,0:T(8,128)S(1)} custom-call(f32[2,128,128]{2,1,0:T(8,128)} %copy-done.8), custom_call_target="InvertDiagBlocksLowerTriangular" | custom-call | tf_op jit(solution)/shard_map/triangular_solve/custom-call.0 | solution.py:23
  570.0 136.1 %all-reduce.12.cloned.1.call-done = f32[256,256]{0,1:T(8,128)} async-done(((f32[256,256]{0,1:T(8,128)}), f32[256,256]{0,1:T(8,128)}) %all-reduce.12.cloned.1.call-update) | async-done | bytes 262160 | tf_op jit(solution)/shard_map/psum | solution.py:11
  706.1 10.2 broadcast_select_fusion
  716.3 178.5 %all-reduce.14.cloned.1.call-done = f32[12,256,256]{1,2,0:T(8,128)} async-done(((f32[12,256,256]{1,2,0:T(8,128)}), f32[12,256,256]{1,2,0:T(8,128)}) %all-reduce.14.cloned.1.call-update) | async-done | bytes 3145744 | tf_op jit(solution)/shard_map/psum | solution.py:11
  899.4 132.2 %all-reduce.16.cloned.1.call-done = f32[256,256]{0,1:T(8,128)} async-done(((f32[256,256]{0,1:T(8,128)}), f32[256,256]{0,1:T(8,128)}) %all-reduce.16.cloned.1.call-update) | async-done | bytes 262160 | tf_op jit(solution)/shard_map/psum | solution.py:11
  1034.4 11.7 cholesky.164
  1046.1 9.8 custom-call.15
  1058.1 11.7 cholesky.181
  1078.5 20.6 %custom-call.16 = f32[2,128,128]{1,2,0:T(8,128)S(1)} custom-call(f32[2,128,128]{2,1,0:T(8,128)} %copy-done.7), custom_call_target="InvertDiagBlocksLowerTriangular" | custom-call | tf_op jit(solution)/shard_map/triangular_solve/custom-call.0 | solution.py:23
  1114.4 136.2 %all-reduce.18.cloned.1.call-done = f32[256,256]{0,1:T(8,128)} async-done(((f32[256,256]{0,1:T(8,128)}), f32[256,256]{0,1:T(8,128)}) %all-reduce.18.cloned.1.call-update) | async-done | bytes 262160 | tf_op jit(solution)/shard_map/psum | solution.py:11
  1250.5 6.0 fusion.7
  (113 shorter events, 85.7 us)
Async XLA Ops:
  25.6 114.7 %all-to-all-start = ((f32[16,2,256,256]{3,1,2,0:T(2,128)}), f32[16,2,256,256]{3,1,2,0:T(2,128)}, u32[]{:S(2)}, u32[]{:S(2)}) async-start(f32[16,2,256,256]{3,1,2,0:T(2,128)} %copy.61), calls=%async_computation | async-start | bytes 16777216 | tf_op jit(solution)/shard_map/all_to_all | solution.py:47
  31.4 310.3 %all-reduce.8.cloned.1.call-start = ((), (), s32[]{:S(2)}) async-start(), calls=%async_computation.1 | async-start | bytes 6291456 | tf_op jit(solution)/shard_map/psum | solution.py:11
  31.5 2.4 copy-start.9
  31.5 3.1 copy-start.10
  162.7 316.3 %all-reduce.10.cloned.1.call-start = ((), (), s32[]{:S(2)}) async-start(), calls=%async_computation.2 | async-start | bytes 524288 | tf_op jit(solution)/shard_map/psum | solution.py:11
  343.4 362.6 %all-reduce.12.cloned.1.call-start = ((), (), s32[]{:S(2)}) async-start(), calls=%async_computation.3 | async-start | bytes 524288 | tf_op jit(solution)/shard_map/psum | solution.py:11
  481.1 0.7 copy-start.5
  517.3 2.6 copy-start.2
  526.3 0.6 copy-start.8
  547.6 3.1 copy-start.1
  567.5 1.7 copy-start
  569.9 324.9 %all-reduce.14.cloned.1.call-start = ((), (), s32[]{:S(2)}) async-start(), calls=%async_computation.4 | async-start | bytes 6291456 | tf_op jit(solution)/shard_map/psum | solution.py:11
  716.3 315.3 %all-reduce.16.cloned.1.call-start = ((), (), s32[]{:S(2)}) async-start(), calls=%async_computation.5 | async-start | bytes 524288 | tf_op jit(solution)/shard_map/psum | solution.py:11
  896.5 354.0 %all-reduce.18.cloned.1.call-start = ((), (), s32[]{:S(2)}) async-start(), calls=%async_computation.6 | async-start | bytes 524288 | tf_op jit(solution)/shard_map/psum | solution.py:11
  1033.7 0.7 copy-start.6
  1069.9 2.4 copy-start.3
  1077.8 0.7 copy-start.7
  1107.5 3.6 copy-start.4
Sparse Core Ops, SparseCore 0:
  162.8 178.9 all-reduce.7
  344.4 134.6 all-reduce.9
  570.0 135.9 all-reduce.11
  716.4 178.3 all-reduce.13
  897.3 134.2 all-reduce.15
  1114.5 136.0 all-reduce.17
where the time goes:
time: 1280 us; the launch traced here: 1270 us
  waiting for transfers between devices  999 us (78%)
  other arithmetic  134 us (10%)
  local copies, waits for them, and re-layouts  55.7 us (4%)
  matrix products  54.7 us (4%)
  between operations  16.6 us (1%)
    psum x6, waiting for transfers between devices, spread(): return lax.psum(block, axis)  893 us
    all_to_all x1, waiting for transfers between devices, per_device(): lax.all_to_all(outgoing, ('sub', 'row'), split_axis=0, concat_axis=0, til...  106 us
    another operation x14, other arithmetic, per_device(): factor = jnp.linalg.cholesky(diag)  69.2 us
    another operation x7, other arithmetic, right_solve(): lax.linalg.triangular_solve(factor, stacked.reshape(-1, tile), left_side=...  47.5 us
  transfers between devices with their start and end apart: 7, of which 7 were waited for; matrix products, arithmetic and copies ran while one was open for 1% of the time, Pallas kernels for 0%

commit v1 on v0

v1 whole, which is shorter than its diff:
```python
import functools

import jax
import jax.numpy as jnp
from jax import lax
from jax.experimental import pallas as pl
from jax.experimental.pallas import tpu as pltpu
from jax.sharding import PartitionSpec as P

MESH = pl.DeviceIdType.MESH
MIB = 1024 * 1024
HIGHEST = lax.Precision.HIGHEST


def tables(rmap, owner_me, frows):
    owners = rmap.shape[2]
    maps = rmap.reshape(-1, owners)
    target = maps % owners
    index = jnp.arange(owners)
    earlier = (target[:, None, :] == target[:, :, None]) & (index[None, None, :] < index[None, :, None])
    rank = jnp.sum(earlier.astype(jnp.int32), axis=2)
    mine = jnp.sum(jnp.where((index == owner_me)[:, None], target, 0), axis=0)
    mine_rank = jnp.sum(jnp.where((index == owner_me)[:, None], rank, 0), axis=0)
    dest = index ^ owner_me
    hit = (mine[None, None, :] == dest[:, None, None]) & (mine_rank[None, None, :] == jnp.arange(2)[None, :, None])
    send = jnp.sum(jnp.where(hit, index[None, None, :], 0), axis=2).reshape(-1)
    place = (index ^ owner_me)[:, None] * 2 + rank
    wanted = jnp.arange(frows) * owners + owner_me
    found = maps.reshape(2, -1)[None] == wanted[:, None, None]
    look = jnp.sum(jnp.where(found, place.reshape(2, -1)[None], 0), axis=2)
    here = jnp.sum(found.astype(jnp.int32), axis=2)
    return send.astype(jnp.int32), look.reshape(-1).astype(jnp.int32), here.reshape(-1).astype(jnp.int32)


def exchange_kernel(
    send_ref, look_ref, here_ref, pattern_ref, initial_ref, child_ref,
    front_ref, cols_ref, lead_ref,
    out_buf, in_buf,
    x_send, x_recv, a_send, a_recv, c_send, c_recv, b_send, b_recv, s_send, s_recv, g_send, g_recv,
):
    rows = lax.axis_size("row")
    owners = lax.axis_size("sub") * rows
    depth = lax.axis_size("col") // 2
    frows, tile = initial_ref.shape[0], initial_ref.shape[2]
    half = tile // 2
    sub, row, col = lax.axis_index("sub"), lax.axis_index("row"), lax.axis_index("col")
    me = sub * rows + row
    z, plane = col // 2, col % 2
    other = 1 - plane

    def peer(delta):
        there = me ^ delta
        return (there // rows, there % rows, col)

    up = (sub, row, ((z + 1) % depth) * 2 + plane)
    down = (sub, row, ((z + depth - 1) % depth) * 2 + plane)
    across = (sub, row, z * 2 + other)
    ways = (up, down)

    barrier = pltpu.get_barrier_semaphore()
    for delta in range(1, owners):
        pl.semaphore_signal(barrier, inc=1, device_id=peer(delta), device_id_type=MESH)
    for there in (up, down, across):
        pl.semaphore_signal(barrier, inc=1, device_id=there, device_id_type=MESH)

    for s in range(2):
        out_buf[s] = child_ref[0, 0, send_ref[s]]

    def fill(delta, carry):
        for s in range(2):
            out_buf[delta * 2 + s] = child_ref[0, 0, send_ref[delta * 2 + s]]
        return carry

    lax.fori_loop(1, owners, fill, 0)
    for s in range(2):
        in_buf[s] = out_buf[s]
    pl.semaphore_wait(barrier, owners - 1 + 3)

    def x_copy(delta):
        part = pl.ds(delta * 2, 2)
        return pltpu.make_async_remote_copy(
            src_ref=out_buf.at[part], dst_ref=in_buf.at[part], send_sem=x_send.at[delta],
            recv_sem=x_recv.at[delta], device_id=peer(delta), device_id_type=MESH,
        )

    for delta in range(1, owners):
        x_copy(delta).start()
    for delta in range(1, owners):
        x_copy(delta).wait_recv()

    def assemble(m, carry):
        value = initial_ref[m, 0] * pattern_ref[m].astype(jnp.float32)
        for c in range(2):
            tile_in = in_buf[look_ref[m * 2 + c]]
            value = value + jnp.where(here_ref[m * 2 + c] > 0, tile_in, 0.0)
        front_ref[m] = value

        @pl.when(z == 0)
        def _():
            cols_ref[plane, m] = value

        return carry

    lax.fori_loop(0, frows, assemble, 0)

    quarter = half // 2

    def a_copy(h, i):
        part = cols_ref.at[plane, i // 2, pl.ds(h * half + (i % 2) * quarter, quarter)]
        return pltpu.make_async_remote_copy(
            src_ref=part, dst_ref=part, send_sem=a_send.at[h, i], recv_sem=a_recv.at[h, i],
            device_id=ways[h], device_id_type=MESH,
        )

    passes_on = (z != depth - 1, z != 1)

    def a_step(i, carry):
        for h in range(2):
            @pl.when(z != 0)
            def _():
                a_copy(h, i).wait_recv()

            @pl.when(passes_on[h])
            def _():
                a_copy(h, i).start()

        return carry

    lax.fori_loop(0, 2 * frows, a_step, 0)

    piece = half // depth
    group = frows // 2

    def cut(k, h, g, origin):
        return cols_ref.at[k, pl.ds(g * group, group), pl.ds(h * half + origin * piece, piece)]

    def c_copy(k, h, g):
        part = cut(k, h, g, z)
        return pltpu.make_async_remote_copy(
            src_ref=part, dst_ref=part, send_sem=c_send.at[h, g], recv_sem=c_recv.at[h, g],
            device_id=across, device_id_type=MESH,
        )

    for g in range(2):
        for h in range(2):
            c_copy(plane, h, g).start()

    def b_copy(h, g, t, origin):
        part = cut(other, h, g, origin)
        return pltpu.make_async_remote_copy(
            src_ref=part, dst_ref=part, send_sem=b_send.at[h, g, t], recv_sem=b_recv.at[h, g, t],
            device_id=ways[h], device_id_type=MESH,
        )

    def origin_of(h, t):
        return (z + depth - t) % depth if h == 0 else (z + t) % depth

    for g in range(2):
        for h in range(2):
            c_copy(other, h, g).wait_recv()
            b_copy(h, g, 0, origin_of(h, 0)).start()

    def b_step(t, carry):
        for g in range(2):
            for h in range(2):
                b_copy(h, g, t - 1, origin_of(h, t)).wait_recv()

                @pl.when(t < depth - 1)
                def _():
                    b_copy(h, g, t, origin_of(h, t)).start()

        return carry

    lax.fori_loop(1, depth, b_step, 0)

    strip = tile // owners
    sources = (0, 1, col % owners)

    def s_copy(s, delta):
        rows_there = pl.ds((me ^ delta) * strip, strip)
        return pltpu.make_async_remote_copy(
            src_ref=cols_ref.at[:, 0, rows_there], dst_ref=lead_ref.at[s, :, rows_there],
            send_sem=s_send.at[s, delta], recv_sem=s_recv.at[s], device_id=peer(delta), device_id_type=MESH,
        )

    for s, source in enumerate(sources):
        @pl.when(me == source)
        def _():
            for delta in range(1, owners):
                s_copy(s, delta).start()
            mine = pl.ds(pl.multiple_of(me * strip, strip), strip)
            lead_ref[s, :, mine] = cols_ref[:, 0, mine]

    def s_arrival(s):
        mine = pl.ds(me * strip, strip)
        return pltpu.make_async_remote_copy(
            src_ref=cols_ref.at[:, 0, mine], dst_ref=lead_ref.at[s, :, mine],
            send_sem=s_send.at[s, 0], recv_sem=s_recv.at[s], device_id=across, device_id_type=MESH,
        )

    for s, source in enumerate(sources):
        @pl.when(me != source)
        def _():
            s_arrival(s).wait_recv()

    def g_copy(delta, holder):
        part = lead_ref.at[:, :, pl.ds(holder * strip, strip)]
        return pltpu.make_async_remote_copy(
            src_ref=part, dst_ref=part, send_sem=g_send.at[delta], recv_sem=g_recv.at[delta],
            device_id=peer(delta), device_id_type=MESH,
        )

    for delta in range(1, owners):
        g_copy(delta, me).start()
    for delta in range(1, owners):
        g_copy(delta, me ^ delta).wait_recv()

    for delta in range(1, owners):
        g_copy(delta, me).wait_send()
        x_copy(delta).wait_send()
    for s, source in enumerate(sources):
        @pl.when(me == source)
        def _():
            for delta in range(1, owners):
                s_copy(s, delta).wait_send()
    for g in range(2):
        for h in range(2):
            c_copy(plane, h, g).wait_send()

    def b_end(t, carry):
        for g in range(2):
            for h in range(2):
                b_copy(h, g, t, origin_of(h, t)).wait_send()
        return carry

    lax.fori_loop(0, depth - 1, b_end, 0)

    def a_end(i, carry):
        for h in range(2):
            @pl.when(passes_on[h])
            def _():
                a_copy(h, i).wait_send()
        return carry

    lax.fori_loop(0, 2 * frows, a_end, 0)


def exchange(initial, pattern, rmap, child_update):
    owners = lax.axis_size("sub") * lax.axis_size("row")
    depth = lax.axis_size("col") // 2
    frows, _, tile, _ = initial.shape
    me = lax.axis_index(("sub", "row"))
    send, look, here = tables(rmap, me, frows)
    smem = pl.BlockSpec(memory_space=pltpu.SMEM)
    vmem = pl.BlockSpec(memory_space=pltpu.VMEM)
    dma = pltpu.SemaphoreType.DMA
    return pl.pallas_call(
        exchange_kernel,
        out_shape=(
            jax.ShapeDtypeStruct((frows, tile, tile), jnp.float32),
            jax.ShapeDtypeStruct((2, frows, tile, tile), jnp.float32),
            jax.ShapeDtypeStruct((3, 2, tile, tile), jnp.float32),
        ),
        in_specs=[smem] * 4 + [vmem] * 2,
        out_specs=(vmem, vmem, vmem),
        scratch_shapes=[
            pltpu.VMEM((2 * owners, tile, tile), jnp.float32),
            pltpu.VMEM((2 * owners, tile, tile), jnp.float32),
            dma((owners,)), dma((owners,)),
            dma((2, 2 * frows)), dma((2, 2 * frows)),
            dma((2, 2)), dma((2, 2)),
            dma((2, 2, depth)), dma((2, 2, depth)),
            dma((3, owners)), dma((3,)),
            dma((owners,)), dma((owners,)),
        ],
        compiler_params=pltpu.CompilerParams(
            collective_id=0, has_side_effects=True, vmem_limit_bytes=56 * MIB
        ),
    )(send, look, here, pattern.reshape(-1), initial, child_update)


def mul(a, b):
    return jnp.dot(a, b, preferred_element_type=jnp.float32, precision=HIGHEST)


def mul_t(a, b):
    return lax.dot_general(
        a, b, (((1,), (1,)), ((), ())), preferred_element_type=jnp.float32, precision=HIGHEST
    )


def factor_block(block):
    n = block.shape[0]
    row_id = lax.broadcasted_iota(jnp.int32, (n, 1), 0)
    eye = (lax.broadcasted_iota(jnp.int32, (n, n), 0) == lax.broadcasted_iota(jnp.int32, (n, n), 1))

    def body(step, carry):
        left, right = carry
        live = row_id < n - 8 * step
        for i in range(8):
            scale = jnp.where((row_id > i) & live, left[:, i:i + 1] / left[i:i + 1, i:i + 1], 0.0)
            left, right = left - scale * left[i:i + 1, :], right - scale * right[i:i + 1, :]
        left = jnp.concatenate([left[8:], left[:8]], axis=0)
        left = pltpu.roll(left, n - 8, 1)
        right = jnp.concatenate([right[8:], right[:8]], axis=0)
        return left, right

    upper, inverse = lax.fori_loop(0, n // 8, body, (block, eye.astype(jnp.float32)))
    scale = lax.rsqrt(jnp.sum(jnp.where(eye, upper, 0.0), axis=1, keepdims=True))
    keep = lax.broadcasted_iota(jnp.int32, (n, n), 0) <= lax.broadcasted_iota(jnp.int32, (n, n), 1)
    return jnp.where(keep, upper * scale, 0.0).T, inverse * scale


def factor_tile(tile_value, factor_ref, inverse_ref):
    n = tile_value.shape[0]
    h = n // 2
    sym = 0.5 * (tile_value + tile_value.T)
    l0, t0 = factor_block(sym[:h, :h])
    l10 = mul_t(sym[h:, :h], t0)
    l1, t1 = factor_block(sym[h:, h:] - mul_t(l10, l10))
    zero = jnp.zeros((h, h), jnp.float32)
    factor_ref[:h, :h] = l0
    factor_ref[:h, h:] = zero
    factor_ref[h:, :h] = l10
    factor_ref[h:, h:] = l1
    inverse_ref[:h, :h] = t0
    inverse_ref[:h, h:] = zero
    inverse_ref[h:, :h] = -mul(t1, mul(l10, t0))
    inverse_ref[h:, h:] = t1


def split(x):
    high = x.astype(jnp.bfloat16)
    return high, (x - high.astype(jnp.float32)).astype(jnp.bfloat16)


def finish_kernel(front_ref, cols_ref, lead_ref, out_ref, f0_ref, i0_ref, f1_ref, i1_ref, own_ref):
    rows = lax.axis_size("row")
    frows, tile = front_ref.shape[0], front_ref.shape[1]
    me = lax.axis_index("sub") * rows + lax.axis_index("row")
    col = lax.axis_index("col")
    eye = (
        lax.broadcasted_iota(jnp.int32, (tile, tile), 0) == lax.broadcasted_iota(jnp.int32, (tile, tile), 1)
    ).astype(jnp.float32)

    factor_tile(lead_ref[0, 0], f0_ref, i0_ref)
    i0 = i0_ref[...]
    l10 = mul_t(lead_ref[1, 0], i0)
    factor_tile(lead_ref[1, 1] - mul_t(l10, l10), f1_ref, i1_ref)
    i1 = i1_ref[...]
    p0 = mul_t(lead_ref[2, 0], i0)
    own_ref[...] = p0
    p1 = mul_t(lead_ref[2, 1] - mul_t(p0, l10), i1)
    p0 = jnp.where(col == 0, eye, jnp.where(col == 1, 0.0, p0))
    p1 = jnp.where(col == 0, 0.0, jnp.where(col == 1, eye, p1))
    n1 = mul(p1, i1)
    n0 = mul(p0 - mul(n1, l10), i0)
    sign = jnp.where(col < 2, 1.0, -1.0)
    keep = jnp.where(col < 2, 0.0, 1.0)
    n0_high, n0_low = split(n0)
    n1_high, n1_low = split(n1)

    def dot_t(a, b):
        return lax.dot_general(a, b, (((1,), (1,)), ((), ())), preferred_element_type=jnp.float32)

    def body(m, carry):
        a0_high, a0_low = split(cols_ref[0, m])
        a1_high, a1_low = split(cols_ref[1, m])
        total = dot_t(a0_low, n0_high) + dot_t(a0_high, n0_low) + dot_t(a1_low, n1_high) + dot_t(a1_high, n1_low)
        total = total + dot_t(a0_high, n0_high) + dot_t(a1_high, n1_high)
        out_ref[m] = keep * front_ref[m] + sign * total
        return carry

    lax.fori_loop(0, frows, body, 0)

    @pl.when(me == 0)
    def _():
        out_ref[0] = jnp.where(col == 0, f0_ref[...], jnp.where(col == 1, 0.0, front_ref[0]))

    @pl.when((me == 1) & (col == 1))
    def _():
        out_ref[0] = f1_ref[...]

    @pl.when((me == 1) & (col > 1))
    def _():
        out_ref[0] = front_ref[0] - mul_t(mul_t(lead_ref[1, 0], i0_ref[...]), own_ref[...])


def finish(front, cols, lead):
    frows, tile, _ = front.shape
    vmem = pl.BlockSpec(memory_space=pltpu.VMEM)
    return pl.pallas_call(
        finish_kernel,
        out_shape=jax.ShapeDtypeStruct(front.shape, jnp.float32),
        in_specs=[vmem] * 3,
        out_specs=vmem,
        scratch_shapes=[pltpu.VMEM((tile, tile), jnp.float32)] * 5,
        compiler_params=pltpu.CompilerParams(vmem_limit_bytes=48 * MIB),
    )(front, cols, lead)


def per_device(initial, pattern, rmap, child_update):
    front, cols, lead = exchange(initial, pattern, rmap, child_update)
    return finish(front, cols, lead)[:, None]


def solution(mesh):
    return jax.shard_map(
        per_device,
        mesh=mesh,
        in_specs=(
            P(None, ("sub", "row"), None, "col"),
            P(None, ("sub", "row"), "col"),
            P(),
            P("sub", "row", None, None, "col"),
        ),
        out_specs=P(None, ("sub", "row"), None, "col"),
        check_vma=False,
    )
```

time: 1280 us -> 1240 us (0.969)
  Pallas kernels: 0 us -> 1220 us
  waiting for transfers between devices: 999 us -> 0 us
  other arithmetic: 134 us -> 2.8 us
  matrix products: 54.7 us -> 0 us
  local copies, waits for them, and re-layouts: 55.7 us -> 6.16 us
  between operations: 16.6 us -> 0.06 us
    pallas_call x0 -> x2, Pallas kernels: none -> 1220 us  [the longest x1 1160 us: exchange(): pl.pallas_call(exchange_kernel, out_shape=(jax.ShapeDtypeStruct((frows, t...]
    psum x6 -> x0, waiting for transfers between devices: 893 us -> none  [spread(): return lax.psum(block, axis)]
    another operation x21 -> x0, other arithmetic: 117 us -> none  [the longest x14 69.2 us: per_device(): factor = jnp.linalg.cholesky(diag)]
    all_to_all x1 -> x0, waiting for transfers between devices: 106 us -> none  [per_device(): lax.all_to_all(outgoing, ('sub', 'row'), split_axis=0, concat_axis=0, til...]
    dot_general x4 -> x0, matrix products: 37.4 us -> none  [the longest x2 16.2 us: per_device(): jnp.einsum('mab,cb->mac', panel, row_tile, precision=lax.Precision.HIGHEST)]
    another operation x10 -> x0, matrix products: 17.4 us -> none  [the longest x6 13.1 us: right_solve(): lax.linalg.triangular_solve(factor, stacked.reshape(-1, tile), left_side=...]
    dot_general x2 -> x0, local copies, waits for them, and re-layouts: 14.6 us -> none  [the longest x1 9.69 us: per_device(): jnp.einsum('dsk,kab->dsab', select, child_update[0, 0], precision=lax.Pre...]
    another operation x21 -> x0, local copies, waits for them, and re-layouts: 14.3 us -> none  [the longest x17 14.3 us: right_solve(): lax.linalg.triangular_solve(factor, stacked.reshape(-1, tile), left_side=...]
  transfers between devices with their start and end apart: 7 -> 0, of which waited for: 7 -> 0; matrix products, arithmetic and copies ran while one was open for 1% -> 0% of each run, Pallas kernels for 0% -> 0%
where the time goes in v1:
time: 1240 us; the launch traced here: 1230 us
  Pallas kernels  1220 us (98%)
    pallas_call x1, Pallas kernels, exchange(): pl.pallas_call(exchange_kernel, out_shape=(jax.ShapeDtypeStruct((frows, t...  1160 us
    pallas_call x1, Pallas kernels, finish(): pl.pallas_call(finish_kernel, out_shape=jax.ShapeDtypeStruct(front.shape,...  63.4 us

profile of v1, /device:TPU:130, one launch (start us, length us, event | category | flops | bytes accessed | tf_op | source)
XLA Modules:
  0.0 1233.5 jit_solution(6865341267486173016)
XLA Ops:
  0.0 0.8 fusion.4
  0.8 0.1 broadcast_compare_fusion
  0.9 0.8 eq.96
  1.7 0.1 add.51
  1.8 0.1 add.52
  1.8 0.7 add_select_fusion
  2.6 0.4 convert_reduce_fusion
  3.0 0.1 select_reduce_fusion.1
  3.1 0.1 reduce_sum.60
  3.2 0.1 select_reduce_fusion
  3.3 0.1 copy.7
  3.4 0.6 reshape.167.send_ref
  4.0 0.5 fusion.1
  4.5 0.6 reshape.169.here_ref
  5.2 0.6 reshape.168.look_ref
  5.7 1161.0 %shard_map.46 = (f32[12,256,256]{2,1,0:T(8,128)}, f32[2,12,256,256]{3,2,1,0:T(8,128)}, f32[3,2,256,256]{3,2,1,0:T(8,128)}) custom-call(s32[32]{0:T(128)} %reshape.167.send_ref, s32[24]{0:T(128)} %reshape.168.look_ref, s32[24]{0:T(128)} %reshape.169.here_ref, s32[12]{0:T(128)} %bitcast.8, f32[12,1,256,256]{3,2,1,0:T(8,128)} %initial_ref.1, ...), custom_call_target="tpu_custom_call" | custom-call | tf_op jit(solution)/shard_map/pallas_call | solution.py:257
  1166.8 0.0 copy-start
  1166.8 1.9 copy-done
  1168.6 0.0 copy-start.1
  1168.6 1.4 copy-done.1
  1170.0 63.4 %shard_map.47 = f32[12,256,256]{2,1,0:T(8,128)} custom-call(f32[12,256,256]{2,1,0:T(8,128)S(1)} %copy-done, f32[2,12,256,256]{3,2,1,0:T(8,128)} %get-tuple-element.9.cols_ref, f32[3,2,256,256]{3,2,1,0:T(8,128)S(1)} %copy-done.1), custom_call_target="tpu_custom_call" | custom-call | tf_op jit(solution)/shard_map/pallas_call | solution.py:392
  (8 shorter events, 0.1 us)
Async XLA Ops:
  1166.8 1.9 copy-start
  1168.6 1.4 copy-start.1

commit v2 on v1

--- a/solution.py
+++ b/solution.py
@@ -112,21 +112,24 @@
             device_id=ways[h], device_id_type=MESH,
         )
 
-    passes_on = (z != depth - 1, z != 1)
-
-    def a_step(i, carry):
+    hops = (z, (depth - z) % depth)
+
+    def a_step(step, carry):
         for h in range(2):
-            @pl.when(z != 0)
+            i = step - hops[h]
+            live = (i >= 0) & (i < 2 * frows)
+
+            @pl.when(live & (z != 0))
             def _():
                 a_copy(h, i).wait_recv()
 
-            @pl.when(passes_on[h])
+            @pl.when(live & (hops[h] != depth - 1))
             def _():
                 a_copy(h, i).start()
 
         return carry
 
-    lax.fori_loop(0, 2 * frows, a_step, 0)
+    lax.fori_loop(0, 2 * frows + depth - 1, a_step, 0)
 
     piece = half // depth
     group = frows // 2
@@ -237,7 +240,7 @@
 
     def a_end(i, carry):
         for h in range(2):
-            @pl.when(passes_on[h])
+            @pl.when(hops[h] != depth - 1)
             def _():
                 a_copy(h, i).wait_send()
         return carry
@@ -274,7 +277,7 @@
             dma((owners,)), dma((owners,)),
         ],
         compiler_params=pltpu.CompilerParams(
-            collective_id=0, has_side_effects=True, vmem_limit_bytes=56 * MIB
+            collective_id=1, has_side_effects=True, vmem_limit_bytes=56 * MIB
         ),
     )(send, look, here, pattern.reshape(-1), initial, child_update)
 
@@ -289,35 +292,48 @@
     )
 
 
-def factor_block(block):
+def factor_block(block, beside=None):
     n = block.shape[0]
-    row_id = lax.broadcasted_iota(jnp.int32, (n, 1), 0)
-    eye = (lax.broadcasted_iota(jnp.int32, (n, n), 0) == lax.broadcasted_iota(jnp.int32, (n, n), 1))
+    width = 16
+    row_id = lax.broadcasted_iota(jnp.int32, (n, n), 0)
+    lane_id = lax.broadcasted_iota(jnp.int32, (n, n), 1)
+    eye = row_id == lane_id
 
     def body(step, carry):
         left, right = carry
-        live = row_id < n - 8 * step
-        for i in range(8):
-            scale = jnp.where((row_id > i) & live, left[:, i:i + 1] / left[i:i + 1, i:i + 1], 0.0)
-            left, right = left - scale * left[i:i + 1, :], right - scale * right[i:i + 1, :]
-        left = jnp.concatenate([left[8:], left[:8]], axis=0)
-        left = pltpu.roll(left, n - 8, 1)
-        right = jnp.concatenate([right[8:], right[:8]], axis=0)
+        if beside is not None:
+            beside(step)
+        live = row_id < n - width * step
+        for i in range(0, width, 2):
+            c0 = jnp.broadcast_to(left[:, i:i + 1], (n, n))
+            c1 = jnp.broadcast_to(left[:, i + 1:i + 2], (n, n))
+            a, b, c = c0[i:i + 1], c0[i + 1:i + 2], c1[i + 1:i + 2]
+            ratio = b / a
+            inv = 1.0 / (c - b * ratio)
+            below = (row_id > i + 1) & live
+            g1 = (c1 - c0 * ratio) * inv
+            g0 = jnp.where(below, c0 / a - g1 * ratio, jnp.where(row_id == i + 1, ratio, 0.0))
+            g1 = jnp.where(below, g1, 0.0)
+            left, right = (
+                left - g0 * left[i:i + 1] - g1 * left[i + 1:i + 2],
+                right - g0 * right[i:i + 1] - g1 * right[i + 1:i + 2],
+            )
+        left = pltpu.roll(jnp.concatenate([left[width:], left[:width]], axis=0), n - width, 1)
+        right = jnp.concatenate([right[width:], right[:width]], axis=0)
         return left, right
 
-    upper, inverse = lax.fori_loop(0, n // 8, body, (block, eye.astype(jnp.float32)))
+    upper, inverse = lax.fori_loop(0, n // width, body, (block, eye.astype(jnp.float32)))
     scale = lax.rsqrt(jnp.sum(jnp.where(eye, upper, 0.0), axis=1, keepdims=True))
-    keep = lax.broadcasted_iota(jnp.int32, (n, n), 0) <= lax.broadcasted_iota(jnp.int32, (n, n), 1)
-    return jnp.where(keep, upper * scale, 0.0).T, inverse * scale
-
-
-def factor_tile(tile_value, factor_ref, inverse_ref):
+    return jnp.where(row_id <= lane_id, upper * scale, 0.0).T, inverse * scale
+
+
+def factor_tile(tile_value, factor_ref, inverse_ref, beside=(None, None)):
     n = tile_value.shape[0]
     h = n // 2
     sym = 0.5 * (tile_value + tile_value.T)
-    l0, t0 = factor_block(sym[:h, :h])
+    l0, t0 = factor_block(sym[:h, :h], beside[0])
     l10 = mul_t(sym[h:, :h], t0)
-    l1, t1 = factor_block(sym[h:, h:] - mul_t(l10, l10))
+    l1, t1 = factor_block(sym[h:, h:] - mul_t(l10, l10), beside[1])
     zero = jnp.zeros((h, h), jnp.float32)
     factor_ref[:h, :h] = l0
     factor_ref[:h, h:] = zero
@@ -399,9 +415,435 @@
     )(front, cols, lead)
 
 
+EXTRA = 2
+
+
+def fast_tables(rmap, me, frows):
+    owners = rmap.shape[2]
+    maps = rmap.reshape(-1, owners)
+    target = maps % owners
+    index = jnp.arange(owners)
+    before = index[None, None, :] < index[None, :, None]
+    rank = jnp.sum(((target[:, None, :] == target[:, :, None]) & before).astype(jnp.int32), axis=2)
+    over = rank > 0
+    order = jnp.sum((over[:, None, :] & before).astype(jnp.int32), axis=2)
+    flat_target, flat_over = target.reshape(-1), over.reshape(-1)
+    flat = jnp.arange(owners * owners)
+    seat = jnp.sum(
+        (
+            (flat_target[None, :] == flat_target[:, None]) & flat_over[None, :] & (flat[None, :] < flat[:, None])
+        ).astype(jnp.int32),
+        axis=1,
+    ).reshape(owners, owners)
+    fits = jnp.max(jnp.where(over, seat, 0)) < EXTRA
+
+    own = (index == me)[:, None]
+    mine = jnp.sum(jnp.where(own, target, 0), axis=0)
+    mine_over = jnp.any(own & over, axis=0)
+    mine_order = jnp.sum(jnp.where(own, order, 0), axis=0)
+    mine_map = jnp.sum(jnp.where(own, maps, 0), axis=0)
+    base_hit = (mine[None, :] == (index ^ me)[:, None]) & ~mine_over[None, :]
+    base = jnp.sum(jnp.where(base_hit, index[None, :], 0), axis=1)
+    over_hit = mine_over[None, :] & (mine_order[None, :] == jnp.arange(2)[:, None])
+    over_index = jnp.sum(jnp.where(over_hit, index[None, :], 0), axis=1)
+    near = (index ^ me)[:, None]
+    spot = (near * 2 + order).reshape(-1)
+    relay_hit = (
+        flat_over[None, None, :]
+        & (flat_target[None, None, :] == (index ^ me)[:, None, None])
+        & (seat.reshape(-1)[None, None, :] == jnp.arange(EXTRA)[None, :, None])
+    )
+    relay = jnp.sum(jnp.where(relay_hit, spot[None, None, :], 0), axis=2).reshape(-1)
+    place = jnp.where(over, owners + seat, near)
+    wanted = jnp.arange(frows) * owners + me
+    found = maps.reshape(2, -1)[None] == wanted[:, None, None]
+    look = jnp.sum(jnp.where(found, place.reshape(2, -1)[None], 0), axis=2).reshape(-1)
+    here = jnp.sum(found.astype(jnp.int32), axis=2).reshape(-1)
+    lead_hit = mine_map[None, :] == jnp.arange(2)[:, None]
+    lead_index = jnp.sum(jnp.where(lead_hit, index[None, :], 0), axis=1)
+    lead_here = jnp.sum(lead_hit.astype(jnp.int32), axis=1)
+    table = jnp.concatenate([base, over_index, relay, lead_index, lead_here, look, here]).astype(jnp.int32)
+    return table, fits
+
+
+def fast_kernel(
+    table_ref, pattern_ref, initial_ref, child_ref, out_ref,
+    out_buf, in_buf, over_src, over_mid, over_out, lead_part, lead_in, lead_strip, lead, cols, own_row,
+    f0_ref, i0_ref, f1_ref, i1_ref, p0_ref,
+    x_send, x_recv, o_send, o_recv, w_send, w_recv, l_send, l_recv, b_send, b_recv, g_send, g_recv,
+    a_send, a_recv, c_send, c_recv, r_send, r_recv, h_send, h_recv,
+):
+    rows = lax.axis_size("row")
+    owners = lax.axis_size("sub") * rows
+    columns = lax.axis_size("col")
+    depth = columns // 2
+    frows, tile = initial_ref.shape[0], initial_ref.shape[2]
+    half, strip = tile // 2, tile // owners
+    sub, row, col = lax.axis_index("sub"), lax.axis_index("row"), lax.axis_index("col")
+    me = sub * rows + row
+    z, plane = col // 2, col % 2
+
+    base_at, over_at = 0, owners
+    relay_at = over_at + 2
+    lead_at = relay_at + owners * EXTRA
+    lead_here_at = lead_at + 2
+    look_at = lead_here_at + 2
+    here_at = look_at + 2 * frows
+
+    def peer(delta):
+        there = me ^ delta
+        return (there // rows, there % rows, col)
+
+    def line(delta):
+        return (sub, row, col ^ delta)
+
+    ways = ((sub, row, ((z + 1) % depth) * 2 + plane), (sub, row, ((z + depth - 1) % depth) * 2 + plane))
+
+    def push(src, dst, send, recv, there):
+        return pltpu.make_async_remote_copy(
+            src_ref=src, dst_ref=dst, send_sem=send, recv_sem=recv, device_id=there, device_id_type=MESH
+        )
+
+    def strip_of(owner):
+        return pl.ds(pl.multiple_of(owner * strip, strip), strip)
+
+    def l_copy(delta):
+        return push(
+            lead_part.at[:, strip_of(me ^ delta)], lead_in.at[delta], l_send.at[delta], l_recv.at[delta], peer(delta)
+        )
+
+    def o_copy(delta):
+        return push(
+            over_src.at[:, strip_of(me ^ delta)], over_mid.at[pl.ds(2 * delta, 2)],
+            o_send.at[delta], o_recv.at[delta], peer(delta),
+        )
+
+    def w_copy(delta, holder):
+        return push(
+            over_out.at[delta], in_buf.at[pl.ds(owners, EXTRA), strip_of(holder)],
+            w_send.at[delta], w_recv.at[delta], peer(delta),
+        )
+
+    def x_copy(delta):
+        return push(out_buf.at[delta], in_buf.at[delta], x_send.at[delta], x_recv.at[delta], peer(delta))
+
+    def b_copy(delta, k):
+        return push(lead_strip, lead.at[k, :, strip_of(me)], b_send.at[delta], b_recv.at[k], line(delta))
+
+    def g_copy(delta, holder):
+        part = lead.at[:, :, strip_of(holder)]
+        return push(part, part, g_send.at[delta], g_recv.at[delta], peer(delta))
+
+    barrier = pltpu.get_barrier_semaphore()
+    for delta in range(1, owners):
+        pl.semaphore_signal(barrier, inc=1, device_id=peer(delta), device_id_type=MESH)
+    for delta in range(1, columns):
+        pl.semaphore_signal(barrier, inc=1, device_id=line(delta), device_id_type=MESH)
+
+    @pl.when(z == 0)
+    def _():
+        for p in range(2):
+            value = jnp.where(table_ref[lead_here_at + p] > 0, child_ref[0, 0, table_ref[lead_at + p]], 0.0)
+            first = initial_ref[0, 0] * pattern_ref[0].astype(jnp.float32)
+            lead_part[p] = value + jnp.where(me == p, first, 0.0)
+
+    for s in range(2):
+        over_src[s] = child_ref[0, 0, table_ref[over_at + s]]
+
+    def fill(delta, carry):
+        out_buf[delta] = child_ref[0, 0, table_ref[base_at + delta]]
+        return carry
+
+    lax.fori_loop(1, owners, fill, 0)
+    in_buf[0] = child_ref[0, 0, table_ref[base_at]]
+    pl.semaphore_wait(barrier, owners - 1 + columns - 1)
+
+    everyone = range(1, owners)
+    first_part, second_part = 4, 8
+
+    @pl.when(z == 0)
+    def _():
+        for delta in everyone:
+            l_copy(delta).start()
+
+    for delta in everyone:
+        o_copy(delta).start()
+    for delta in range(1, min(first_part, owners)):
+        x_copy(delta).start()
+
+    @pl.when(z == 0)
+    def _():
+        total = lead_part[:, strip_of(me)]
+        for delta in everyone:
+            l_copy(delta).wait_recv()
+            total = total + lead_in[delta]
+        lead_strip[...] = total
+        lead[plane, :, strip_of(me)] = total
+        for delta in range(1, columns):
+            b_copy(delta, plane).start()
+
+    for delta in everyone:
+        o_copy(delta).wait_recv()
+    for s in range(2):
+        over_mid[s] = over_src[s, strip_of(me)]
+
+    def relay(delta, carry):
+        for e in range(EXTRA):
+            over_out[delta, e] = over_mid[table_ref[relay_at + delta * EXTRA + e]]
+        return carry
+
+    lax.fori_loop(0, owners, relay, 0)
+    for e in range(EXTRA):
+        in_buf[owners + e, strip_of(me)] = over_out[0, e]
+    for delta in everyone:
+        w_copy(delta, me).start()
+    for delta in range(first_part, min(second_part, owners)):
+        x_copy(delta).start()
+    for k in range(2):
+        @pl.when(col != k)
+        def _():
+            b_copy(0, k).wait_recv()
+    for delta in everyone:
+        g_copy(delta, me).start()
+    for delta in range(second_part, owners):
+        x_copy(delta).start()
+    for delta in everyone:
+        g_copy(delta, me ^ delta).wait_recv()
+
+    factor_tile(lead[0, 0], f0_ref, i0_ref)
+
+    def tiles_arrive():
+        for delta in everyone:
+            x_copy(delta).wait_recv()
+            w_copy(delta, me ^ delta).wait_recv()
+
+    def assembled(m):
+        value = initial_ref[m, 0] * pattern_ref[m].astype(jnp.float32)
+        for c in range(2):
+            tile_in = in_buf[table_ref[look_at + m * 2 + c]]
+            value = value + jnp.where(table_ref[here_at + m * 2 + c] > 0, tile_in, 0.0)
+        return value
+
+    @pl.when(z == 0)
+    def _():
+        tiles_arrive()
+
+        def body(m, carry):
+            cols[plane, m] = assembled(m)
+            return carry
+
+        lax.fori_loop(0, frows, body, 0)
+
+    quarter = half // 2
+    units = 2 * frows
+    hops = (z, (depth - z) % depth)
+
+    def unit(k, h, i):
+        return cols.at[k, i // 2, pl.ds(h * half + (i % 2) * quarter, quarter)]
+
+    def a_copy(h, i):
+        part = unit(plane, h, i)
+        return push(part, part, a_send.at[h, i], a_recv.at[h, i], ways[h])
+
+    def c_copy(k, h, i):
+        part = unit(k, h, i)
+        return push(part, part, c_send.at[h, i], c_recv.at[h, i], line(1))
+
+    def a_step(step):
+        for h in range(2):
+            i = step - hops[h]
+            live = (i >= 0) & (i < units)
+
+            @pl.when(live & (z != 0))
+            def _():
+                a_copy(h, i).wait_recv()
+
+            @pl.when(live & (hops[h] != depth - 1))
+            def _():
+                a_copy(h, i).start()
+
+            @pl.when(live)
+            def _():
+                c_copy(plane, h, i).start()
+
+    def a_steps(start, stop):
+        def body(step, carry):
+            a_step(step)
+            return carry
+
+        lax.fori_loop(start, stop, body, 0)
+
+    i0 = i0_ref[...]
+    l10 = mul_t(lead[0, 1], i0)
+    factor_tile(lead[1, 1] - mul_t(l10, l10), f1_ref, i1_ref, (a_step, lambda step: a_step(step + 8)))
+
+    steps = units + depth - 1
+    done = 2 * (half // 16)
+    for i in range(2):
+        for h in range(2):
+            c_copy(1 - plane, h, i).wait_recv()
+
+    def r_copy(delta):
+        there = strip_of(me ^ delta)
+        return push(cols.at[:, 0, there], own_row.at[:, there], r_send.at[delta], r_recv.at[0], peer(delta))
+
+    @pl.when(me == col)
+    def _():
+        for delta in everyone:
+            r_copy(delta).start()
+        own_row[:, strip_of(me)] = cols[:, 0, strip_of(me)]
+
+    middle = done + (steps - done) // 2
+    late = steps - 4
+    a_steps(done, middle)
+
+    @pl.when(me != col)
+    def _():
+        mine = strip_of(me)
+        push(cols.at[:, 0, mine], own_row.at[:, mine], r_send.at[0], r_recv.at[0], line(1)).wait_recv()
+
+    def h_copy(delta, holder):
+        part = own_row.at[:, strip_of(holder)]
+        return push(part, part, h_send.at[delta], h_recv.at[delta], peer(delta))
+
+    for delta in everyone:
+        h_copy(delta, me).start()
+    a_steps(middle, late)
+    for delta in everyone:
+        h_copy(delta, me ^ delta).wait_recv()
+
+    eye = (
+        lax.broadcasted_iota(jnp.int32, (tile, tile), 0) == lax.broadcasted_iota(jnp.int32, (tile, tile), 1)
+    ).astype(jnp.float32)
+    i1 = i1_ref[...]
+    p0 = mul_t(own_row[0], i0)
+    p0_ref[...] = p0
+    p1 = mul_t(own_row[1] - mul_t(p0, l10), i1)
+    p0 = jnp.where(col == 0, eye, jnp.where(col == 1, 0.0, p0))
+    p1 = jnp.where(col == 0, 0.0, jnp.where(col == 1, eye, p1))
+    n1 = mul(p1, i1)
+    n0 = mul(p0 - mul(n1, l10), i0)
+    sign = jnp.where(col < 2, 1.0, -1.0)
+    keep = jnp.where(col < 2, 0.0, 1.0)
+    n0_high, n0_low = split(n0)
+    n1_high, n1_low = split(n1)
+    a_steps(late, steps)
+
+    @pl.when(z != 0)
+    def _():
+        tiles_arrive()
+
+    def crossed(i, carry):
+        for h in range(2):
+            c_copy(1 - plane, h, i).wait_recv()
+        return carry
+
+    lax.fori_loop(2, units, crossed, 0)
+
+    def dot_t(a, b):
+        return lax.dot_general(a, b, (((1,), (1,)), ((), ())), preferred_element_type=jnp.float32)
+
+    def body(m, carry):
+        a0_high, a0_low = split(cols[0, m])
+        a1_high, a1_low = split(cols[1, m])
+        total = dot_t(a0_low, n0_high) + dot_t(a0_high, n0_low) + dot_t(a1_low, n1_high) + dot_t(a1_high, n1_low)
+        total = total + dot_t(a0_high, n0_high) + dot_t(a1_high, n1_high)
+        out_ref[m] = keep * assembled(m) + sign * total
+        return carry
+
+    lax.fori_loop(0, frows, body, 0)
+
+    @pl.when(me == 0)
+    def _():
+        out_ref[0] = jnp.where(col == 0, f0_ref[...], jnp.where(col == 1, 0.0, assembled(0)))
+
+    @pl.when((me == 1) & (col == 1))
+    def _():
+        out_ref[0] = f1_ref[...]
+
+    @pl.when((me == 1) & (col > 1))
+    def _():
+        out_ref[0] = assembled(0) - mul_t(l10, p0_ref[...])
+
+    @pl.when(z == 0)
+    def _():
+        for delta in everyone:
+            l_copy(delta).wait_send()
+        for delta in range(1, columns):
+            b_copy(delta, plane).wait_send()
+
+    for delta in everyone:
+        o_copy(delta).wait_send()
+        w_copy(delta, me).wait_send()
+        x_copy(delta).wait_send()
+        g_copy(delta, me).wait_send()
+        h_copy(delta, me).wait_send()
+
+    @pl.when(me == col)
+    def _():
+        for delta in everyone:
+            r_copy(delta).wait_send()
+
+    def sent(i, carry):
+        for h in range(2):
+            @pl.when(hops[h] != depth - 1)
+            def _():
+                a_copy(h, i).wait_send()
+
+            c_copy(plane, h, i).wait_send()
+        return carry
+
+    lax.fori_loop(0, units, sent, 0)
+
+
+def fast(table, pattern, initial, child_update):
+    owners = lax.axis_size("sub") * lax.axis_size("row")
+    columns = lax.axis_size("col")
+    frows, _, tile, _ = initial.shape
+    strip, units = tile // owners, 2 * frows
+    smem = pl.BlockSpec(memory_space=pltpu.SMEM)
+    vmem = pl.BlockSpec(memory_space=pltpu.VMEM)
+    dma = pltpu.SemaphoreType.DMA
+
+    def room(*shape):
+        return pltpu.VMEM(shape, jnp.float32)
+
+    return pl.pallas_call(
+        fast_kernel,
+        out_shape=jax.ShapeDtypeStruct((frows, tile, tile), jnp.float32),
+        in_specs=[smem] * 2 + [vmem] * 2,
+        out_specs=vmem,
+        scratch_shapes=[
+            room(owners, tile, tile), room(owners + EXTRA, tile, tile),
+            room(2, tile, tile), room(2 * owners, strip, tile), room(owners, EXTRA, strip, tile),
+            room(2, tile, tile), room(owners, 2, strip, tile), room(2, strip, tile), room(2, 2, tile, tile),
+            room(2, frows, tile, tile), room(2, tile, tile),
+        ] + [room(tile, tile)] * 5 + [
+            dma((owners,)), dma((owners,)), dma((owners,)), dma((owners,)), dma((owners,)), dma((owners,)),
+            dma((owners,)), dma((owners,)), dma((columns,)), dma((2,)), dma((owners,)), dma((owners,)),
+            dma((2, units)), dma((2, units)), dma((2, units)), dma((2, units)),
+            dma((owners,)), dma((1,)), dma((owners,)), dma((owners,)),
+        ],
+        compiler_params=pltpu.CompilerParams(
+            collective_id=0, has_side_effects=True, vmem_limit_bytes=56 * MIB
+        ),
+    )(table, pattern.reshape(-1), initial, child_update)
+
+
+def general(table, pattern, initial, child_update, rmap):
+    return finish(*exchange(initial, pattern, rmap, child_update))
+
+
 def per_device(initial, pattern, rmap, child_update):
-    front, cols, lead = exchange(initial, pattern, rmap, child_update)
-    return finish(front, cols, lead)[:, None]
+    me = lax.axis_index(("sub", "row"))
+    table, fits = fast_tables(rmap, me, initial.shape[0])
+    out = lax.cond(
+        fits,
+        lambda table, pattern, initial, child_update, rmap: fast(table, pattern, initial, child_update),
+        general,
+        table, pattern, initial, child_update, rmap,
+    )
+    return out[:, None]
 
 
 def solution(mesh):

time: 1240 us -> 232 us (0.19)
  the two profiles are of different devices: /device:TPU:130 before, /device:TPU:32 now
where the time goes in v2:
time: 232 us; the launch traced here: 231 us
  Pallas kernels  222 us (96%)
  other arithmetic  4.56 us (2%)
  local copies, waits for them, and re-layouts  4.13 us (2%)
    pallas_call x1, Pallas kernels, fast(): pl.pallas_call(fast_kernel, out_shape=jax.ShapeDtypeStruct((frows, tile,...  222 us

profile of v2, /device:TPU:32, one launch (start us, length us, event | category | flops | bytes accessed | tf_op | source)
XLA Modules:
  0.0 231.5 jit_solution(9361568011011540751)
XLA Ops:
  0.0 0.8 select_reduce_fusion.3
  0.8 0.1 convert_reduce_fusion.4
  1.0 0.8 reshape.475
  1.8 0.8 eq.244
  2.6 0.1 eq.249
  2.7 0.7 add_select_fusion.3
  3.4 0.4 convert_reduce_fusion.3
  3.9 0.1 and_reduce_fusion
  4.0 0.1 gt.31
  4.1 0.2 select_reduce_fusion.5
  4.2 0.1 gt.32
  4.3 0.2 convert_reduce_fusion.1
  4.6 0.3 convert_reduce_fusion.2
  5.0 0.1 broadcast_add_fusion
  5.2 0.1 select_reduce_fusion.2
  5.3 0.1 fusion.14
  5.4 0.1 copy.10
  5.5 0.1 reshape.476
  5.7 0.6 select_reduce_fusion.6
  7.0 0.5 fusion.9
  7.5 0.1 reshape.478
  7.8 222.0 %conditional.1 = (f32[12,1,256,256]{3,2,1,0:T(8,128)S(1)}) conditional(s32[]{:T(128)} %convert_element_type.26, (s32[2,8,16]{2,1,0:T(8,128)}, s32[12,1,1]{0,2,1:T(1,128)}, f32[12,1,256,256]{3,2,1,0:T(8,128)}, f32[1,1,16,256,256]{4,3,2,1,0:T(8,128)}) %tuple.13, (s32[12,1,1]{0,2,1:T(1,128)}, s32[102]{0:T(128)S(1)}, f32[12,1,256,256]{3,2,1,0:T(8,128)}, ...), branch_computations={%region_15.22_spmd, %region_22.23_spmd} | conditional | flops 40544 | bytes 18895948 | solution.py:840
  7.9 221.7 %branch_1_fun.1 = f32[12,256,256]{2,1,0:T(8,128)S(1)} custom-call(s32[102]{0:T(128)S(1)} %get-tuple-element.32.table_ref, s32[12]{0:T(128)} %bitcast.21, f32[12,1,256,256]{3,2,1,0:T(8,128)} %get-tuple-element.34.initial_ref, f32[1,1,16,256,256]{4,3,2,1,0:T(8,128)} %get-tuple-element.35.child_ref), custom_call_target="tpu_custom_call" | custom-call | tf_op jit(solution)/shard_map/cond/branch_1_fun/pallas_call | solution.py:811
  229.8 1.7 copy.17
  (16 shorter events, 0.5 us)

commit v3 on v2

--- a/solution.py
+++ b/solution.py
@@ -416,6 +416,7 @@
 
 
 EXTRA = 2
+SLABS = 4
 
 
 def fast_tables(rmap, me, frows):
@@ -468,7 +469,7 @@
 
 def fast_kernel(
     table_ref, pattern_ref, initial_ref, child_ref, out_ref,
-    out_buf, in_buf, over_src, over_mid, over_out, lead_part, lead_in, lead_strip, lead, cols, own_row,
+    out_buf, in_0, in_1, in_2, in_3, over_in, over_src, over_mid, over_out, lead_part, lead_in, lead_strip, lead, cols, own_row,
     f0_ref, i0_ref, f1_ref, i1_ref, p0_ref,
     x_send, x_recv, o_send, o_recv, w_send, w_recv, l_send, l_recv, b_send, b_recv, g_send, g_recv,
     a_send, a_recv, c_send, c_recv, r_send, r_recv, h_send, h_recv,
@@ -478,7 +479,8 @@
     columns = lax.axis_size("col")
     depth = columns // 2
     frows, tile = initial_ref.shape[0], initial_ref.shape[2]
-    half, strip = tile // 2, tile // owners
+    half, strip, slab = tile // 2, tile // owners, tile // SLABS
+    in_slabs = (in_0, in_1, in_2, in_3)
     sub, row, col = lax.axis_index("sub"), lax.axis_index("row"), lax.axis_index("col")
     me = sub * rows + row
     z, plane = col // 2, col % 2
@@ -520,12 +522,15 @@
 
     def w_copy(delta, holder):
         return push(
-            over_out.at[delta], in_buf.at[pl.ds(owners, EXTRA), strip_of(holder)],
+            over_out.at[delta], over_in.at[:, strip_of(holder)],
             w_send.at[delta], w_recv.at[delta], peer(delta),
         )
 
-    def x_copy(delta):
-        return push(out_buf.at[delta], in_buf.at[delta], x_send.at[delta], x_recv.at[delta], peer(delta))
+    def x_copy(delta, c):
+        part = pl.ds(c * slab, slab)
+        return push(
+            out_buf.at[delta, part], in_slabs[c].at[delta], x_send.at[c, delta], x_recv.at[c, delta], peer(delta)
+        )
 
     def b_copy(delta, k):
         return push(lead_strip, lead.at[k, :, strip_of(me)], b_send.at[delta], b_recv.at[k], line(delta))
@@ -555,12 +560,11 @@
         return carry
 
     lax.fori_loop(1, owners, fill, 0)
-    in_buf[0] = child_ref[0, 0, table_ref[base_at]]
+    for c in range(SLABS):
+        in_slabs[c][0] = child_ref[0, 0, table_ref[base_at], pl.ds(c * slab, slab)]
     pl.semaphore_wait(barrier, owners - 1 + columns - 1)
 
     everyone = range(1, owners)
-    first_part, second_part = 4, 8
-
     @pl.when(z == 0)
     def _():
         for delta in everyone:
@@ -568,8 +572,8 @@
 
     for delta in everyone:
         o_copy(delta).start()
-    for delta in range(1, min(first_part, owners)):
-        x_copy(delta).start()
+    for delta in everyone:
+        x_copy(delta, 0).start()
 
     @pl.when(z == 0)
     def _():
@@ -594,94 +598,120 @@
 
     lax.fori_loop(0, owners, relay, 0)
     for e in range(EXTRA):
-        in_buf[owners + e, strip_of(me)] = over_out[0, e]
+        over_in[e, strip_of(me)] = over_out[0, e]
     for delta in everyone:
         w_copy(delta, me).start()
-    for delta in range(first_part, min(second_part, owners)):
-        x_copy(delta).start()
+    for delta in everyone:
+        x_copy(delta, 1).start()
     for k in range(2):
         @pl.when(col != k)
         def _():
             b_copy(0, k).wait_recv()
     for delta in everyone:
         g_copy(delta, me).start()
-    for delta in range(second_part, owners):
-        x_copy(delta).start()
+    for c in range(2, SLABS):
+        for delta in everyone:
+            x_copy(delta, c).start()
+
+    def slab_arrives(c):
+        for delta in everyone:
+            x_copy(delta, c).wait_recv()
+            if c == 0:
+                w_copy(delta, me ^ delta).wait_recv()
+
+    def assembled_slab(m, c):
+        part = pl.ds(c * slab, slab)
+        value = initial_ref[m, 0, part] * pattern_ref[m].astype(jnp.float32)
+        for child in range(2):
+            spot = table_ref[look_at + m * 2 + child]
+            direct = in_slabs[c][jnp.minimum(spot, owners - 1)]
+            relayed = over_in[jnp.maximum(spot - owners, 0), part]
+            tile_in = jnp.where(spot < owners, direct, relayed)
+            value = value + jnp.where(table_ref[here_at + m * 2 + child] > 0, tile_in, 0.0)
+        return value
+
+    def assembled(m):
+        return jnp.concatenate([assembled_slab(m, c) for c in range(SLABS)], axis=0)
+
+    def each(start, stop, do):
+        def body(i, carry):
+            do(i)
+            return carry
+
+        lax.fori_loop(start, stop, body, 0)
+
+    def root_slab(c):
+        slab_arrives(c)
+        part = pl.ds(c * slab, slab)
+
+        def fill_column(m):
+            cols[plane, m, part] = assembled_slab(m, c)
+
+        each(0, frows, fill_column)
+
+    units = SLABS * frows
+    turn = depth // 2
+    feeds = (z < turn, (z == 0) | (z > turn + 1))
+
+    def unit(k, i):
+        third = i < 3 * frows + 1
+        lead_unit = i < 2 * frows + 2
+        c = jnp.where(i < 2 * frows, i // frows, jnp.where(lead_unit, i - 2 * frows + 2, jnp.where(third, 2, 3)))
+        m = jnp.where(
+            i < 2 * frows, i % frows,
+            jnp.where(lead_unit, 0, jnp.where(third, i - 2 * frows - 1, i - 3 * frows)),
+        )
+        return cols.at[k, m, pl.ds(pl.multiple_of(c * slab, slab), slab)]
+
+    def a_copy(h, i):
+        part = unit(plane, i)
+        return push(part, part, a_send.at[h, i], a_recv.at[i], ways[h])
+
+    def c_copy(k, i):
+        part = unit(k, i)
+        return push(part, part, c_send.at[i], c_recv.at[i], line(1))
+
+    def a_step(i):
+        @pl.when(z != 0)
+        def _():
+            a_copy(0, i).wait_recv()
+
+        for h in range(2):
+            @pl.when(feeds[h])
+            def _():
+                a_copy(h, i).start()
+
+        c_copy(plane, i).start()
+
+    turns = half // 16
+    ahead = units - 4 * turns
+
+    def gate(c, ready):
+        @pl.when(ready & (z == 0))
+        def _():
+            root_slab(c)
+
+    def beside(block):
+        def do(step):
+            i = ahead + block * turns + step
+            for c, first in ((2, 2 * frows), (3, 2 * frows + 1)):
+                if ahead + block * turns <= first < ahead + (block + 1) * turns:
+                    gate(c, i == first)
+            a_step(i)
+
+        return do
+
+    gate(0, True)
+    each(0, frows, a_step)
+    gate(1, True)
+    each(frows, ahead, a_step)
     for delta in everyone:
         g_copy(delta, me ^ delta).wait_recv()
-
-    factor_tile(lead[0, 0], f0_ref, i0_ref)
-
-    def tiles_arrive():
-        for delta in everyone:
-            x_copy(delta).wait_recv()
-            w_copy(delta, me ^ delta).wait_recv()
-
-    def assembled(m):
-        value = initial_ref[m, 0] * pattern_ref[m].astype(jnp.float32)
-        for c in range(2):
-            tile_in = in_buf[table_ref[look_at + m * 2 + c]]
-            value = value + jnp.where(table_ref[here_at + m * 2 + c] > 0, tile_in, 0.0)
-        return value
-
-    @pl.when(z == 0)
-    def _():
-        tiles_arrive()
-
-        def body(m, carry):
-            cols[plane, m] = assembled(m)
-            return carry
-
-        lax.fori_loop(0, frows, body, 0)
-
-    quarter = half // 2
-    units = 2 * frows
-    hops = (z, (depth - z) % depth)
-
-    def unit(k, h, i):
-        return cols.at[k, i // 2, pl.ds(h * half + (i % 2) * quarter, quarter)]
-
-    def a_copy(h, i):
-        part = unit(plane, h, i)
-        return push(part, part, a_send.at[h, i], a_recv.at[h, i], ways[h])
-
-    def c_copy(k, h, i):
-        part = unit(k, h, i)
-        return push(part, part, c_send.at[h, i], c_recv.at[h, i], line(1))
-
-    def a_step(step):
-        for h in range(2):
-            i = step - hops[h]
-            live = (i >= 0) & (i < units)
-
-            @pl.when(live & (z != 0))
-            def _():
-                a_copy(h, i).wait_recv()
-
-            @pl.when(live & (hops[h] != depth - 1))
-            def _():
-                a_copy(h, i).start()
-
-            @pl.when(live)
-            def _():
-                c_copy(plane, h, i).start()
-
-    def a_steps(start, stop):
-        def body(step, carry):
-            a_step(step)
-            return carry
-
-        lax.fori_loop(start, stop, body, 0)
-
-    i0 = i0_ref[...]
-    l10 = mul_t(lead[0, 1], i0)
-    factor_tile(lead[1, 1] - mul_t(l10, l10), f1_ref, i1_ref, (a_step, lambda step: a_step(step + 8)))
-
-    steps = units + depth - 1
-    done = 2 * (half // 16)
-    for i in range(2):
-        for h in range(2):
-            c_copy(1 - plane, h, i).wait_recv()
+    factor_tile(lead[0, 0], f0_ref, i0_ref, (beside(0), beside(1)))
+
+    early = (0, frows, 2 * frows, 2 * frows + 1)
+    for i in early:
+        c_copy(1 - plane, i).wait_recv()
 
     def r_copy(delta):
         there = strip_of(me ^ delta)
@@ -693,22 +723,29 @@
             r_copy(delta).start()
         own_row[:, strip_of(me)] = cols[:, 0, strip_of(me)]
 
-    middle = done + (steps - done) // 2
-    late = steps - 4
-    a_steps(done, middle)
-
-    @pl.when(me != col)
-    def _():
-        mine = strip_of(me)
-        push(cols.at[:, 0, mine], own_row.at[:, mine], r_send.at[0], r_recv.at[0], line(1)).wait_recv()
+    i0 = i0_ref[...]
+    l10 = mul_t(lead[0, 1], i0)
 
     def h_copy(delta, holder):
         part = own_row.at[:, strip_of(holder)]
         return push(part, part, h_send.at[delta], h_recv.at[delta], peer(delta))
 
-    for delta in everyone:
-        h_copy(delta, me).start()
-    a_steps(middle, late)
+    def spread_row(step):
+        @pl.when(step == 0)
+        def _():
+            @pl.when(me != col)
+            def _():
+                mine = strip_of(me)
+                push(
+                    cols.at[:, 0, mine], own_row.at[:, mine], r_send.at[0], r_recv.at[0], line(1)
+                ).wait_recv()
+
+            for delta in everyone:
+                h_copy(delta, me).start()
+
+        beside(3)(step)
+
+    factor_tile(lead[1, 1] - mul_t(l10, l10), f1_ref, i1_ref, (beside(2), spread_row))
     for delta in everyone:
         h_copy(delta, me ^ delta).wait_recv()
 
@@ -727,31 +764,29 @@
     keep = jnp.where(col < 2, 0.0, 1.0)
     n0_high, n0_low = split(n0)
     n1_high, n1_low = split(n1)
-    a_steps(late, steps)
 
     @pl.when(z != 0)
     def _():
-        tiles_arrive()
-
-    def crossed(i, carry):
-        for h in range(2):
-            c_copy(1 - plane, h, i).wait_recv()
-        return carry
-
-    lax.fori_loop(2, units, crossed, 0)
+        for c in range(SLABS):
+            slab_arrives(c)
 
     def dot_t(a, b):
         return lax.dot_general(a, b, (((1,), (1,)), ((), ())), preferred_element_type=jnp.float32)
 
-    def body(m, carry):
+    def update(m):
         a0_high, a0_low = split(cols[0, m])
         a1_high, a1_low = split(cols[1, m])
         total = dot_t(a0_low, n0_high) + dot_t(a0_high, n0_low) + dot_t(a1_low, n1_high) + dot_t(a1_high, n1_low)
         total = total + dot_t(a0_high, n0_high) + dot_t(a1_high, n1_high)
         out_ref[m] = keep * assembled(m) + sign * total
-        return carry
-
-    lax.fori_loop(0, frows, body, 0)
+
+    def last(m):
+        for start in (0, frows, 2 * frows + 1, 3 * frows):
+            c_copy(1 - plane, start + m).wait_recv()
+        update(m)
+
+    update(0)
+    each(1, frows, last)
 
     @pl.when(me == 0)
     def _():
@@ -775,7 +810,8 @@
     for delta in everyone:
         o_copy(delta).wait_send()
         w_copy(delta, me).wait_send()
-        x_copy(delta).wait_send()
+        for c in range(SLABS):
+            x_copy(delta, c).wait_send()
         g_copy(delta, me).wait_send()
         h_copy(delta, me).wait_send()
 
@@ -784,23 +820,22 @@
         for delta in everyone:
             r_copy(delta).wait_send()
 
-    def sent(i, carry):
+    def sent(i):
         for h in range(2):
-            @pl.when(hops[h] != depth - 1)
+            @pl.when(feeds[h])
             def _():
                 a_copy(h, i).wait_send()
 
-            c_copy(plane, h, i).wait_send()
-        return carry
-
-    lax.fori_loop(0, units, sent, 0)
+        c_copy(plane, i).wait_send()
+
+    each(0, units, sent)
 
 
 def fast(table, pattern, initial, child_update):
     owners = lax.axis_size("sub") * lax.axis_size("row")
     columns = lax.axis_size("col")
     frows, _, tile, _ = initial.shape
-    strip, units = tile // owners, 2 * frows
+    strip, units = tile // owners, SLABS * frows
     smem = pl.BlockSpec(memory_space=pltpu.SMEM)
     vmem = pl.BlockSpec(memory_space=pltpu.VMEM)
     dma = pltpu.SemaphoreType.DMA
@@ -814,14 +849,14 @@
         in_specs=[smem] * 2 + [vmem] * 2,
         out_specs=vmem,
         scratch_shapes=[
-            room(owners, tile, tile), room(owners + EXTRA, tile, tile),
+            room(owners, tile, tile), *[room(owners, tile // SLABS, tile)] * SLABS, room(EXTRA, tile, tile),
             room(2, tile, tile), room(2 * owners, strip, tile), room(owners, EXTRA, strip, tile),
             room(2, tile, tile), room(owners, 2, strip, tile), room(2, strip, tile), room(2, 2, tile, tile),
             room(2, frows, tile, tile), room(2, tile, tile),
         ] + [room(tile, tile)] * 5 + [
-            dma((owners,)), dma((owners,)), dma((owners,)), dma((owners,)), dma((owners,)), dma((owners,)),
+            dma((SLABS, owners)), dma((SLABS, owners)), dma((owners,)), dma((owners,)), dma((owners,)), dma((owners,)),
             dma((owners,)), dma((owners,)), dma((columns,)), dma((2,)), dma((owners,)), dma((owners,)),
-            dma((2, units)), dma((2, units)), dma((2, units)), dma((2, units)),
+            dma((2, units)), dma((units,)), dma((units,)), dma((units,)),
             dma((owners,)), dma((1,)), dma((owners,)), dma((owners,)),
         ],
         compiler_params=pltpu.CompilerParams(

time: 232 us -> 189 us (0.81)
  the two profiles are of different devices: /device:TPU:32 before, /device:TPU:130 now
where the time goes in v3:
time: 189 us
  Pallas kernels  179 us (95%)
  other arithmetic  4.56 us (2%)
  local copies, waits for them, and re-layouts  4.13 us (2%)
    pallas_call x1, Pallas kernels, fast(): pl.pallas_call(fast_kernel, out_shape=jax.ShapeDtypeStruct((frows, tile,...  179 us

profile of v3, /device:TPU:130, one launch (start us, length us, event | category | flops | bytes accessed | tf_op | source)
XLA Modules:
  0.0 188.9 jit_solution(8157090996545522382)
XLA Ops:
  0.0 0.8 select_reduce_fusion.3
  0.8 0.1 convert_reduce_fusion.4
  1.0 0.8 reshape.475
  1.8 0.8 eq.244
  2.6 0.1 eq.249
  2.7 0.7 add_select_fusion.3
  3.4 0.4 convert_reduce_fusion.3
  3.9 0.1 and_reduce_fusion
  4.0 0.1 gt.31
  4.1 0.2 select_reduce_fusion.5
  4.2 0.1 gt.32
  4.3 0.2 convert_reduce_fusion.1
  4.6 0.3 convert_reduce_fusion.2
  5.0 0.1 broadcast_add_fusion
  5.2 0.1 select_reduce_fusion.2
  5.3 0.1 fusion.14
  5.4 0.1 copy.10
  5.5 0.1 reshape.476
  5.7 0.6 select_reduce_fusion.6
  7.0 0.5 fusion.9
  7.5 0.1 reshape.478
  7.8 179.4 %conditional.1 = (f32[12,1,256,256]{3,2,1,0:T(8,128)S(1)}) conditional(s32[]{:T(128)} %convert_element_type.26, (s32[2,8,16]{2,1,0:T(8,128)}, s32[12,1,1]{0,2,1:T(1,128)}, f32[12,1,256,256]{3,2,1,0:T(8,128)}, f32[1,1,16,256,256]{4,3,2,1,0:T(8,128)}) %tuple.13, (s32[12,1,1]{0,2,1:T(1,128)}, s32[102]{0:T(128)S(1)}, f32[12,1,256,256]{3,2,1,0:T(8,128)}, ...), branch_computations={%region_15.22_spmd, %region_22.23_spmd} | conditional | flops 40544 | bytes 18895948 | solution.py:875
  7.9 179.1 %branch_1_fun.1 = f32[12,256,256]{2,1,0:T(8,128)S(1)} custom-call(s32[102]{0:T(128)S(1)} %get-tuple-element.32.table_ref, s32[12]{0:T(128)} %bitcast.21, f32[12,1,256,256]{3,2,1,0:T(8,128)} %get-tuple-element.34.initial_ref, f32[1,1,16,256,256]{4,3,2,1,0:T(8,128)} %get-tuple-element.35.child_ref), custom_call_target="tpu_custom_call" | custom-call | tf_op jit(solution)/shard_map/cond/branch_1_fun/pallas_call | solution.py:846
  187.2 1.7 copy.17
  (16 shorter events, 0.5 us)

commit v4 on v3

--- a/solution.py
+++ b/solution.py
@@ -417,6 +417,8 @@
 
 EXTRA = 2
 SLABS = 4
+RETURNED = 2
+LAG = 6
 
 
 def fast_tables(rmap, me, frows):
@@ -472,7 +474,7 @@
     out_buf, in_0, in_1, in_2, in_3, over_in, over_src, over_mid, over_out, lead_part, lead_in, lead_strip, lead, cols, own_row,
     f0_ref, i0_ref, f1_ref, i1_ref, p0_ref,
     x_send, x_recv, o_send, o_recv, w_send, w_recv, l_send, l_recv, b_send, b_recv, g_send, g_recv,
-    a_send, a_recv, c_send, c_recv, r_send, r_recv, h_send, h_recv,
+    a_send, a_recv, c_send, c_recv, d_send, d_recv, r_send, r_recv, h_send, h_recv,
 ):
     rows = lax.axis_size("row")
     owners = lax.axis_size("sub") * rows
@@ -484,6 +486,7 @@
     sub, row, col = lax.axis_index("sub"), lax.axis_index("row"), lax.axis_index("col")
     me = sub * rows + row
     z, plane = col // 2, col % 2
+    other = 1 - plane
 
     base_at, over_at = 0, owners
     relay_at = over_at + 2
@@ -671,6 +674,43 @@
         part = unit(k, i)
         return push(part, part, c_send.at[i], c_recv.at[i], line(1))
 
+    def d_copy(h, i):
+        part = unit(other, i)
+        return push(part, part, d_send.at[h, i], d_recv.at[i], ways[h])
+
+    def bridge(i):
+        return turn + i % 2
+
+    def returns(i):
+        return (i < RETURNED * frows) & (i % frows != 0)
+
+    def crosses(i):
+        return jnp.logical_not(returns(i)) | (z == bridge(i))
+
+    def goes(i):
+        up = ((z > turn) & (z < depth - 1)) | ((z == turn) & (bridge(i) == turn))
+        down = ((z >= 1) & (z <= turn)) | ((z == turn + 1) & (bridge(i) == turn + 1))
+        return up, down
+
+    behinds = (
+        4 + LAG * jnp.abs(z - turn),
+        jnp.where(z > turn, 4 + LAG * (z - turn - 1), 5 + LAG * (turn - z)),
+    )
+
+    def d_step(i):
+        @pl.when(z == bridge(i))
+        def _():
+            c_copy(other, i).wait_recv()
+
+        @pl.when(z != bridge(i))
+        def _():
+            d_copy(0, i).wait_recv()
+
+        for h, goes_on in enumerate(goes(i)):
+            @pl.when(goes_on)
+            def _():
+                d_copy(h, i).start()
+
     def a_step(i):
         @pl.when(z != 0)
         def _():
@@ -681,7 +721,19 @@
             def _():
                 a_copy(h, i).start()
 
-        c_copy(plane, i).start()
+        @pl.when(crosses(i))
+        def _():
+            c_copy(plane, i).start()
+
+        way_back(i)
+
+    def way_back(i):
+        for odd, behind in enumerate(behinds):
+            back = i - behind
+
+            @pl.when((back >= 0) & (back % 2 == odd) & returns(back))
+            def _():
+                d_step(back)
 
     turns = half // 16
     ahead = units - 4 * turns
@@ -746,6 +798,7 @@
         beside(3)(step)
 
     factor_tile(lead[1, 1] - mul_t(l10, l10), f1_ref, i1_ref, (beside(2), spread_row))
+    each(units, RETURNED * frows + 6 + LAG * turn, way_back)
     for delta in everyone:
         h_copy(delta, me ^ delta).wait_recv()
 
@@ -781,8 +834,8 @@
         out_ref[m] = keep * assembled(m) + sign * total
 
     def last(m):
-        for start in (0, frows, 2 * frows + 1, 3 * frows):
-            c_copy(1 - plane, start + m).wait_recv()
+        for start in (2 * frows + 1, 3 * frows):
+            c_copy(other, start + m).wait_recv()
         update(m)
 
     update(0)
@@ -826,7 +879,14 @@
             def _():
                 a_copy(h, i).wait_send()
 
-        c_copy(plane, i).wait_send()
+        @pl.when(crosses(i))
+        def _():
+            c_copy(plane, i).wait_send()
+
+        for h, goes_on in enumerate(goes(i)):
+            @pl.when(goes_on & returns(i))
+            def _():
+                d_copy(h, i).wait_send()
 
     each(0, units, sent)
 
@@ -856,7 +916,7 @@
         ] + [room(tile, tile)] * 5 + [
             dma((SLABS, owners)), dma((SLABS, owners)), dma((owners,)), dma((owners,)), dma((owners,)), dma((owners,)),
             dma((owners,)), dma((owners,)), dma((columns,)), dma((2,)), dma((owners,)), dma((owners,)),
-            dma((2, units)), dma((units,)), dma((units,)), dma((units,)),
+            dma((2, units)), dma((units,)), dma((units,)), dma((units,)), dma((2, units)), dma((units,)),
             dma((owners,)), dma((1,)), dma((owners,)), dma((owners,)),
         ],
         compiler_params=pltpu.CompilerParams(

time: 189 us -> 175 us (0.926)
  Pallas kernels: 179 us -> 164 us
    pallas_call x1, Pallas kernels: 179 us -> 164 us  [fast(): pl.pallas_call(fast_kernel, out_shape=jax.ShapeDtypeStruct((frows, tile,...]
where the time goes in v4:
time: 175 us; the launch traced here: 174 us
  Pallas kernels  164 us (94%)
  other arithmetic  4.56 us (3%)
  local copies, waits for them, and re-layouts  4.13 us (2%)
    pallas_call x1, Pallas kernels, fast(): pl.pallas_call(fast_kernel, out_shape=jax.ShapeDtypeStruct((frows, tile,...  164 us

profile of v4, /device:TPU:130, one launch (start us, length us, event | category | flops | bytes accessed | tf_op | source)
XLA Modules:
  0.0 174.2 jit_solution(12479919981893670223)
XLA Ops:
  0.0 0.8 select_reduce_fusion.3
  0.8 0.1 convert_reduce_fusion.4
  1.0 0.8 reshape.475
  1.8 0.8 eq.244
  2.6 0.1 eq.249
  2.7 0.7 add_select_fusion.3
  3.4 0.4 convert_reduce_fusion.3
  3.9 0.1 and_reduce_fusion
  4.0 0.1 gt.31
  4.1 0.2 select_reduce_fusion.5
  4.2 0.1 gt.32
  4.3 0.2 convert_reduce_fusion.1
  4.6 0.3 convert_reduce_fusion.2
  5.0 0.1 broadcast_add_fusion
  5.2 0.1 select_reduce_fusion.2
  5.3 0.1 fusion.14
  5.4 0.1 copy.10
  5.5 0.1 reshape.476
  5.7 0.6 select_reduce_fusion.6
  7.0 0.5 fusion.9
  7.5 0.1 reshape.478
  7.8 164.8 %conditional.1 = (f32[12,1,256,256]{3,2,1,0:T(8,128)S(1)}) conditional(s32[]{:T(128)} %convert_element_type.26, (s32[2,8,16]{2,1,0:T(8,128)}, s32[12,1,1]{0,2,1:T(1,128)}, f32[12,1,256,256]{3,2,1,0:T(8,128)}, f32[1,1,16,256,256]{4,3,2,1,0:T(8,128)}) %tuple.13, (s32[12,1,1]{0,2,1:T(1,128)}, s32[102]{0:T(128)S(1)}, f32[12,1,256,256]{3,2,1,0:T(8,128)}, ...), branch_computations={%region_15.22_spmd, %region_22.23_spmd} | conditional | flops 40544 | bytes 18895948 | solution.py:935
  7.9 164.4 %branch_1_fun.1 = f32[12,256,256]{2,1,0:T(8,128)S(1)} custom-call(s32[102]{0:T(128)S(1)} %get-tuple-element.32.table_ref, s32[12]{0:T(128)} %bitcast.21, f32[12,1,256,256]{3,2,1,0:T(8,128)} %get-tuple-element.34.initial_ref, f32[1,1,16,256,256]{4,3,2,1,0:T(8,128)} %get-tuple-element.35.child_ref), custom_call_target="tpu_custom_call" | custom-call | tf_op jit(solution)/shard_map/cond/branch_1_fun/pallas_call | solution.py:906
  172.5 1.7 copy.17
  (16 shorter events, 0.5 us)

commit v5 on v4

--- a/solution.py
+++ b/solution.py
@@ -418,7 +418,7 @@
 EXTRA = 2
 SLABS = 4
 RETURNED = 2
-LAG = 6
+LAG = 8
 
 
 def fast_tables(rmap, me, frows):

time: 175 us -> 170 us (0.971)
  Pallas kernels: 164 us -> 159 us
    pallas_call x1, Pallas kernels: 164 us -> 159 us  [fast(): pl.pallas_call(fast_kernel, out_shape=jax.ShapeDtypeStruct((frows, tile,...]
where the time goes in v5:
time: 170 us; the launch traced here: 169 us
  Pallas kernels  159 us (94%)
  other arithmetic  4.56 us (3%)
  local copies, waits for them, and re-layouts  4.13 us (2%)
    pallas_call x1, Pallas kernels, fast(): pl.pallas_call(fast_kernel, out_shape=jax.ShapeDtypeStruct((frows, tile,...  159 us

profile of v5, /device:TPU:130, one launch (start us, length us, event | category | flops | bytes accessed | tf_op | source)
XLA Modules:
  0.0 169.2 jit_solution(16941358316013629613)
XLA Ops:
  0.0 0.8 select_reduce_fusion.3
  0.8 0.1 convert_reduce_fusion.4
  1.0 0.8 reshape.475
  1.8 0.8 eq.244
  2.6 0.1 eq.249
  2.7 0.7 add_select_fusion.3
  3.4 0.4 convert_reduce_fusion.3
  3.9 0.1 and_reduce_fusion
  4.0 0.1 gt.31
  4.1 0.2 select_reduce_fusion.5
  4.2 0.1 gt.32
  4.3 0.2 convert_reduce_fusion.1
  4.6 0.3 convert_reduce_fusion.2
  5.0 0.1 broadcast_add_fusion
  5.2 0.1 select_reduce_fusion.2
  5.3 0.1 fusion.14
  5.4 0.1 copy.10
  5.5 0.1 reshape.476
  5.7 0.6 select_reduce_fusion.6
  7.0 0.5 fusion.9
  7.5 0.1 reshape.478
  7.8 159.8 %conditional.1 = (f32[12,1,256,256]{3,2,1,0:T(8,128)S(1)}) conditional(s32[]{:T(128)} %convert_element_type.26, (s32[2,8,16]{2,1,0:T(8,128)}, s32[12,1,1]{0,2,1:T(1,128)}, f32[12,1,256,256]{3,2,1,0:T(8,128)}, f32[1,1,16,256,256]{4,3,2,1,0:T(8,128)}) %tuple.13, (s32[12,1,1]{0,2,1:T(1,128)}, s32[102]{0:T(128)S(1)}, f32[12,1,256,256]{3,2,1,0:T(8,128)}, ...), branch_computations={%region_15.22_spmd, %region_22.23_spmd} | conditional | flops 40544 | bytes 18895948 | solution.py:935
  7.9 159.4 %branch_1_fun.1 = f32[12,256,256]{2,1,0:T(8,128)S(1)} custom-call(s32[102]{0:T(128)S(1)} %get-tuple-element.32.table_ref, s32[12]{0:T(128)} %bitcast.21, f32[12,1,256,256]{3,2,1,0:T(8,128)} %get-tuple-element.34.initial_ref, f32[1,1,16,256,256]{4,3,2,1,0:T(8,128)} %get-tuple-element.35.child_ref), custom_call_target="tpu_custom_call" | custom-call | tf_op jit(solution)/shard_map/cond/branch_1_fun/pallas_call | solution.py:906
  167.6 1.7 copy.17
  (16 shorter events, 0.5 us)
